TPU v7x, 128 devices: a whole 4x4x4 slice. The times are simulated.
128 devices in a mesh: rows: 32 (over z, y, core), group: 4 (over x).
Axes of the slice: x: 4, y: 4, z: 4, core: 2. Of those that a mesh axis runs over, the one named last changes fastest.
Arguments:
- slab: float32 [786432, 512], P(('rows', 'group')), may hold values from -16 to 16
Outputs:
- updated: float32 [786432, 512], P(('rows', 'group'))
All inputs are finite; a program needn't handle non-finite values.
Results may differ from a plain program's by a relative error of at most 0.0001.
Values sent between devices are 32-bit elements; how exact they have to be, the bound alone decides.
A program may use at most 128 MiB of HBM per device.

v0:
```python
import math

import jax
import jax.numpy as jnp
from jax import lax
from jax.sharding import PartitionSpec as P

lower_bound = 0.1
spread_d = (4.0 * (1.0 - lower_bound**2) / lower_bound**4) ** (1.0 / 3.0)
weight_alpha = math.sqrt(1.0 + spread_d) + 0.5 * math.sqrt(
    8.0
    - 4.0 * spread_d
    + 8.0 * (2.0 - lower_bound**2) / (lower_bound**2 * math.sqrt(1.0 + spread_d))
)
weight_beta = (weight_alpha - 1.0) ** 2 / 4.0
weight_gamma = weight_alpha + weight_beta - 1.0


def cross_product(left, right):
    return lax.dot_general(
        left,
        right,
        (((0,), (0,)), ((), ())),
        precision=lax.Precision.HIGHEST,
        preferred_element_type=jnp.float32,
    )


def local(slab):
    width = slab.shape[1]
    devices_all = lax.axis_size("rows") * lax.axis_size("group")
    total_rows = slab.shape[0] * devices_all
    scale = weight_gamma / total_rows
    identity = jnp.eye(width, dtype=jnp.float32)
    partial_gram = cross_product(slab, slab)
    within = lax.psum(partial_gram, "rows")
    summed = lax.psum(within, "group")
    lower = jnp.linalg.cholesky(scale * summed + identity)
    inverse_low = lax.linalg.triangular_solve(lower, identity, left_side=True, lower=True)
    inverse = cross_product(inverse_low, inverse_low)
    mixing = (
        weight_beta / weight_gamma * identity
        + (weight_alpha - weight_beta / weight_gamma) * inverse
    )
    return jnp.dot(
        slab, mixing, precision=lax.Precision.HIGHEST, preferred_element_type=jnp.float32
    )


def solution(mesh):
    placed = (P(("rows", "group"), None),)
    return jax.shard_map(
        local, mesh=mesh, in_specs=placed, out_specs=P(("rows", "group"), None), check_vma=False
    )
```

profile of v0, /device:TPU:1, one launch (start us, length us, event | category | flops | bytes accessed | tf_op | source)
XLA Modules:
  0.0 382.8 jit_solution(18171631885099615969)
XLA Ops:
  6.5 26.1 %fusion.41 = f32[512,512]{0,1:T(8,128)} fusion(f32[6144,512]{1,0:T(8,128)} %param.1), kind=kOutput, calls=%fused_computation.80 | convolution fusion | flops 19327352832 | bytes 13631488 | tf_op jit(solution)/shard_map/dot_general | solution.py:20
  32.9 108.1 %all-reduce.4.cloned.1.call-done = f32[512,512]{0,1:T(8,128)} async-done(((f32[512,512]{0,1:T(8,128)}), f32[512,512]{0,1:T(8,128)}) %all-reduce.4.cloned.1.call-update) | async-done | bytes 1048592 | tf_op jit(solution)/shard_map/psum | solution.py:36
  141.1 0.8 iota_compare_fusion.1
  142.0 45.7 %all-reduce.6.cloned.1.call-done = f32[512,512]{0,1:T(8,128)} async-done(((f32[512,512]{0,1:T(8,128)}), f32[512,512]{0,1:T(8,128)}) %all-reduce.6.cloned.1.call-update) | async-done | bytes 1048592 | tf_op jit(solution)/shard_map/psum | solution.py:37
  187.6 1.4 multiply_add_fusion
  189.3 1.5 fusion.8
  190.8 11.7 %cholesky.103 = f32[128,128]{1,0:T(8,128)S(1)} custom-call(f32[128,128]{1,0:T(8,128)S(1)} %cholesky.263), custom_call_target="Cholesky" | custom-call | tf_op jit(solution)/shard_map/jit(cholesky)/cholesky | solution.py:38
  202.5 0.7 copy.4
  203.3 9.8 %custom-call.30 = f32[1,128,128]{1,2,0:T(8,128)S(1)} custom-call(f32[1,128,128]{2,1,0:T(8,128)S(1)} %get-tuple-element.32), custom_call_target="InvertDiagBlocksLowerTriangular" | custom-call | tf_op jit(solution)/shard_map/jit(cholesky)/cholesky | solution.py:38
  213.9 11.7 %cholesky.215 = f32[128,128]{1,0:T(8,128)S(1)} custom-call(f32[128,128]{1,0:T(8,128)S(1)} %cholesky.267), custom_call_target="Cholesky" | custom-call | tf_op jit(solution)/shard_map/jit(cholesky)/cholesky | solution.py:38
  225.6 0.7 copy.6
  226.4 10.6 %custom-call.31 = f32[1,128,128]{1,2,0:T(8,128)} custom-call(f32[1,128,128]{2,1,0:T(8,128)S(1)} %get-tuple-element.30), custom_call_target="InvertDiagBlocksLowerTriangular" | custom-call | tf_op jit(solution)/shard_map/jit(cholesky)/cholesky | solution.py:38
  237.0 1.0 cholesky.222
  238.0 0.8 constant_dynamic-update-slice_fusion.2
  238.8 1.2 convolution_dynamic-update-slice_fusion
  240.6 11.7 %cholesky.236 = f32[128,128]{1,0:T(8,128)S(1)} custom-call(f32[128,128]{1,0:T(8,128)S(1)} %cholesky.272), custom_call_target="Cholesky" | custom-call | tf_op jit(solution)/shard_map/jit(cholesky)/cholesky | solution.py:38
  252.4 9.8 %custom-call.32 = f32[1,128,128]{1,2,0:T(8,128)S(1)} custom-call(f32[1,128,128]{2,1,0:T(8,128)S(1)} %get-tuple-element.28), custom_call_target="InvertDiagBlocksLowerTriangular" | custom-call | tf_op jit(solution)/shard_map/jit(cholesky)/cholesky | solution.py:38
  263.0 12.1 %cholesky.253 = f32[128,128]{1,0:T(8,128)S(1)} custom-call(f32[128,128]{1,0:T(8,128)S(1)} %convolution_subtract_fusion.5), custom_call_target="Cholesky" | custom-call | tf_op jit(solution)/shard_map/jit(cholesky)/cholesky | solution.py:38
  275.3 0.7 compare_reduce_fusion.1
  276.6 0.7 compare_reduce_fusion.2
  280.0 11.0 %while.1 = (s32[]{:T(128)}, f32[512,512]{0,1:T(8,128)S(1)}, s32[4,2]{0,1:T(2,128)S(1)}, f32[4,128,128]{2,1,0:T(8,128)}, s32[]{:T(128)}) while((s32[]{:T(128)}, f32[512,512]{0,1:T(8,128)S(1)}, s32[4,2]{0,1:T(2,128)S(1)}, f32[4,128,128]{2,1,0:T(8,128)}, s32[]{:T(128)}) %tuple.24), condition=%wide.while_cond, body=%wide.while_body.sunk | while | flops 2 | bytes 393329 | solution.py:39
  280.7 1.3 dynamic-slice.7
  283.4 1.3 dynamic-slice.7
  286.2 1.3 dynamic-slice.7
  288.9 1.3 dynamic-slice.7
  291.0 40.1 %custom-call.33 = f32[4,128,128]{1,2,0:T(8,128)S(1)} custom-call(f32[4,128,128]{2,1,0:T(8,128)} %get-tuple-element.12), custom_call_target="InvertDiagBlocksLowerTriangular" | custom-call | tf_op jit(solution)/shard_map/triangular_solve | solution.py:39
  331.1 1.1 fusion.19
  333.2 1.0 convolution_subtract_fusion
  334.7 1.5 convolution_subtract_fusion.2
  336.6 1.9 fusion
  338.5 24.7 %convolution_bitcast_fusion = f32[6144,512]{0,1:T(8,128)} fusion(f32[512,512]{0,1:T(8,128)S(1)} %fusion, f32[6144,512]{1,0:T(8,128)} %param.1), kind=kOutput, calls=%fused_computation.2 | convolution fusion | flops 19327352832 | bytes 26214400 | tf_op jit(solution)/shard_map/dot_general | solution.py:45
  363.2 12.6 %copy.12 = f32[6144,512]{1,0:T(8,128)} copy(f32[6144,512]{0,1:T(8,128)} %convolution_bitcast_fusion) | data formatting | bytes 25165824 | tf_op jit(solution)/shard_map/dot_general | solution.py:45
  (49 shorter events, 11.4 us)
Async XLA Ops:
  6.5 134.5 %all-reduce.4.cloned.1.call-start = ((), (), s32[]{:S(2)}) async-start(), calls=%async_computation | async-start | bytes 2097152 | tf_op jit(solution)/shard_map/psum | solution.py:36
  32.7 154.9 %all-reduce.6.cloned.1.call-start = ((), (), s32[]{:S(2)}) async-start(), calls=%async_computation.1 | async-start | bytes 2097152 | tf_op jit(solution)/shard_map/psum | solution.py:37
Sparse Core Ops, SparseCore 0:
  32.8 108.1 all-reduce.3
  143.5 44.0 all-reduce.5
where the time goes:
time: 388 us; the launch traced here: 383 us
  waiting for transfers between devices  154 us (40%)
  other arithmetic  124 us (32%)
  matrix products  61.4 us (16%)
  local copies, waits for them, and re-layouts  27.5 us (7%)
  between operations  16.4 us (4%)
    psum x1, waiting for transfers between devices, local(): within = lax.psum(partial_gram, 'rows')  108 us
    another operation x14, other arithmetic, local(): lower = jnp.linalg.cholesky(scale * summed + identity)  79.6 us
    psum x1, waiting for transfers between devices, local(): summed = lax.psum(within, 'group')  45.7 us
    another operation x3, other arithmetic, local(): lax.linalg.triangular_solve(lower, identity, left_side=True, lower=True)  40.3 us
    dot_general x2, matrix products, cross_product(): lax.dot_general(left, right, (((0,), (0,)), ((), ())), precision=lax.Prec...  28.1 us
    dot_general x1, matrix products, local(): jnp.dot(slab, mixing, precision=lax.Precision.HIGHEST, preferred_element_...  24.7 us
    dot_general x1, local copies, waits for them, and re-layouts, local(): jnp.dot(slab, mixing, precision=lax.Precision.HIGHEST, preferred_element_...  12.6 us
    another operation x20, local copies, waits for them, and re-layouts  10.9 us
  transfers between devices with their start and end apart: 2, of which 2 were waited for; matrix products, arithmetic and copies ran while one was open for 0% of the time, Pallas kernels for 0%

commit v1 on v0

v1 whole, which is shorter than its diff:
```python
import functools
import math

import jax
import jax.numpy as jnp
from jax import lax
from jax.experimental import pallas as pl
from jax.experimental.pallas import tpu as pltpu
from jax.sharding import PartitionSpec as P

lower_bound = 0.1
spread_d = (4.0 * (1.0 - lower_bound**2) / lower_bound**4) ** (1.0 / 3.0)
weight_alpha = math.sqrt(1.0 + spread_d) + 0.5 * math.sqrt(
    8.0
    - 4.0 * spread_d
    + 8.0 * (2.0 - lower_bound**2) / (lower_bound**2 * math.sqrt(1.0 + spread_d))
)
weight_beta = (weight_alpha - 1.0) ** 2 / 4.0
weight_gamma = weight_alpha + weight_beta - 1.0

MESH = pl.DeviceIdType.MESH
SIDE = 4
PLANE = SIDE * SIDE
BLOCK = 128
TILE = 8
CHUNK = 512
BLOCKS = [
    (0, 0), (0, 1), (0, 2), (0, 3), (1, 1),
    (1, 2), (1, 3), (2, 2), (2, 3), (3, 3),
]
HALF = 5 * BLOCK // TILE
STREAMS = [("xy", "z", 2, 0), ("yz", "x", 2, 32), ("zx", "y", 1, 64)]
VMEM_BYTES = 56 * 2**20
SHIFTS = [(i, j) for i in range(SIDE) for j in range(SIDE) if i or j]
GOOD = 8e-3

f32, bf16 = jnp.float32, jnp.bfloat16


def dot(left, right):
    return jnp.dot(left, right, preferred_element_type=f32)


def cross(left, right):
    return lax.dot_general(left, right, (((0,), (0,)), ((), ())), preferred_element_type=f32)


def split(value):
    high = value.astype(bf16)
    return high, (value - high.astype(f32)).astype(bf16)


def dot_three(left, right):
    left_high, left_low = split(left)
    right_high, right_low = split(right)
    return dot(left_high, right_high) + (dot(left_high, right_low) + dot(left_low, right_high))


def gram_kernel(
    slab, out, held, partial, packed, core_in, rs_a, rs_b, rs_c, ln_a, ln_b, ln_c, mine_a, mine_b,
    mine_c, full, load_sem, core_sem, rs_send, rs_recv, ln_send, ln_recv, ag_send, ag_recv,
):
    rows = slab.shape[0]
    index = lax.axis_index("rows")
    core = lax.rem(index, 2)
    here = {
        "x": lax.axis_index("group"),
        "y": lax.rem(lax.div(index, 2), SIDE),
        "z": lax.div(index, 2 * SIDE),
    }

    def device(shift):
        at = {name: lax.rem(here[name] + shift.get(name, 0), SIDE) for name in here}
        return ((at["z"] * SIDE + at["y"]) * 2 + core, at["x"])

    sibling = (index + 1 - 2 * core, here["x"])

    def load(i):
        part = pl.ds(i * CHUNK, CHUNK)
        return pltpu.make_async_copy(slab.at[part], held.at[part], load_sem.at[i])

    for i in range(rows // CHUNK):
        load(i).start()

    barrier = pltpu.get_barrier_semaphore()
    shifts = []
    for plane, _, _, _ in STREAMS:
        for i, j in SHIFTS:
            shift = {plane[0]: i, plane[1]: j}
            shift = tuple((name, shift[name]) for name in "xyz" if shift.get(name, 0))
            if shift not in shifts:
                shifts.append(shift)
    for shift in shifts:
        pl.semaphore_signal(barrier, inc=1, device_id=device(dict(shift)), device_id_type=MESH)
    pl.semaphore_signal(barrier, inc=1, device_id=sibling, device_id_type=MESH)

    for i in range(rows // CHUNK):
        load(i).wait()
        block = held[pl.ds(i * CHUNK, CHUNK), :]
        high = block.astype(bf16)
        low = ((block - high.astype(f32)) * 2.0).astype(bf16)
        term = cross(jnp.concatenate([high, high], 0), jnp.concatenate([high, low], 0))
        partial[...] = term if i == 0 else partial[...] + term

    for n, (i, j) in enumerate(BLOCKS):
        a = partial[i * BLOCK : (i + 1) * BLOCK, j * BLOCK : (j + 1) * BLOCK]
        b = partial[j * BLOCK : (j + 1) * BLOCK, i * BLOCK : (i + 1) * BLOCK]
        packed[n // 5, pl.ds((n % 5) * PLANE, PLANE)] = (a + b.T).reshape(PLANE, TILE, BLOCK)

    pl.semaphore_wait(barrier, len(shifts) + 1)

    give = pltpu.make_async_remote_copy(
        src_ref=packed.at[1 - core], dst_ref=core_in, send_sem=core_sem.at[0],
        recv_sem=core_sem.at[1], device_id=sibling, device_id_type=MESH,
    )
    give.start()
    give.wait()
    packed[core] = packed[core] + core_in[...]

    rs, ln, mine = (rs_a, rs_b, rs_c), (ln_a, ln_b, ln_c), (mine_a, mine_b, mine_c)
    spots = [here[plane[0]] * SIDE + here[plane[1]] for plane, _, _, _ in STREAMS]

    for s, (plane, _, units, first) in enumerate(STREAMS):
        for k, (i, j) in enumerate(SHIFTS):
            spot = lax.rem(here[plane[0]] + i, SIDE) * SIDE + lax.rem(here[plane[1]] + j, SIDE)
            pltpu.make_async_remote_copy(
                src_ref=packed.at[core, pl.ds(first + units * spot, units)], dst_ref=rs[s].at[k],
                send_sem=rs_send.at[s], recv_sem=rs_recv.at[s],
                device_id=device({plane[0]: i, plane[1]: j}), device_id_type=MESH,
            ).start()
    for s, (plane, line, units, first) in enumerate(STREAMS):
        pltpu.make_async_copy(rs[s], rs[s], rs_recv.at[s]).wait()
        mine[s][...] = packed[core, pl.ds(first + units * spots[s], units)] + jnp.sum(rs[s][...], axis=0)
        for k in range(SIDE - 1):
            pltpu.make_async_remote_copy(
                src_ref=mine[s], dst_ref=ln[s].at[k], send_sem=ln_send.at[s],
                recv_sem=ln_recv.at[s], device_id=device({line: k + 1}), device_id_type=MESH,
            ).start()
    for s, (plane, line, units, first) in enumerate(STREAMS):
        pltpu.make_async_copy(ln[s], ln[s], ln_recv.at[s]).wait()
        place = full.at[core, pl.ds(first + units * spots[s], units)]
        place[...] = mine[s][...] + jnp.sum(ln[s][...], axis=0)
        for i, j in SHIFTS:
            pltpu.make_async_remote_copy(
                src_ref=place, dst_ref=place, send_sem=ag_send.at[s], recv_sem=ag_recv.at[s],
                device_id=device({plane[0]: i, plane[1]: j}), device_id_type=MESH,
            ).start()
    for s, (plane, line, units, first) in enumerate(STREAMS):
        got = full.at[core, pl.ds(first, (PLANE - 1) * units)]
        pltpu.make_async_copy(got, got, ag_recv.at[s]).wait()
    back = pltpu.make_async_remote_copy(
        src_ref=full.at[core], dst_ref=full.at[core], send_sem=core_sem.at[2],
        recv_sem=core_sem.at[3], device_id=sibling, device_id_type=MESH,
    )
    back.start()
    for s, (plane, line, units, first) in enumerate(STREAMS):
        sent = full.at[core, pl.ds(first, (PLANE - 1) * units)]
        pltpu.make_async_copy(rs[s], rs[s], rs_send.at[s]).wait()
        pltpu.make_async_copy(ln[s], ln[s], ln_send.at[s]).wait()
        pltpu.make_async_copy(sent, sent, ag_send.at[s]).wait()
    back.wait()
    out[...] = full[...]


def reduced_gram(slab):
    rows, width = slab.shape
    unit = lambda *lead: pltpu.VMEM((*lead, TILE, BLOCK), f32)
    dma = pltpu.SemaphoreType.DMA
    return pl.pallas_call(
        gram_kernel,
        out_shape=jax.ShapeDtypeStruct((2, HALF, TILE, BLOCK), f32),
        in_specs=[pl.BlockSpec(memory_space=pl.ANY)],
        out_specs=pl.BlockSpec(memory_space=pltpu.VMEM),
        scratch_shapes=[
            pltpu.VMEM((rows, width), f32),
            pltpu.VMEM((width, width), f32),
            unit(2, HALF),
            unit(HALF),
            *[unit(PLANE - 1, units) for _, _, units, _ in STREAMS],
            *[unit(SIDE - 1, units) for _, _, units, _ in STREAMS],
            *[unit(units) for _, _, units, _ in STREAMS],
            unit(2, HALF),
            dma((rows // CHUNK,)),
            dma((4,)),
            *[dma((3,)) for _ in range(6)],
        ],
        compiler_params=pltpu.CompilerParams(
            collective_id=0, has_side_effects=True, vmem_limit_bytes=VMEM_BYTES
        ),
    )(slab)


def apply_kernel(
    scale, gram, slab, out, held, ready, shifted, work, mixing, load_sem, store_sem
):
    rows, width = slab.shape

    def load(i):
        part = pl.ds(i * CHUNK, CHUNK)
        return pltpu.make_async_copy(slab.at[part], held.at[part], load_sem.at[i])

    def store(i):
        part = pl.ds(i * CHUNK, CHUNK)
        return pltpu.make_async_copy(ready.at[part], out.at[part], store_sem.at[i])

    for i in range(rows // CHUNK):
        load(i).start()

    row_ids = lax.broadcasted_iota(jnp.int32, (width, width), 0)
    col_ids = lax.broadcasted_iota(jnp.int32, (width, width), 1)
    identity = (row_ids == col_ids).astype(f32)
    for n, (i, j) in enumerate(BLOCKS):
        a = gram[n // 5, pl.ds((n % 5) * PLANE, PLANE)].reshape(BLOCK, BLOCK)
        shifted[i * BLOCK : (i + 1) * BLOCK, j * BLOCK : (j + 1) * BLOCK] = a
        if i != j:
            shifted[j * BLOCK : (j + 1) * BLOCK, i * BLOCK : (i + 1) * BLOCK] = a.T
    matrix = shifted[...] * scale + identity

    diagonal = matrix * identity
    diagonal_row = jnp.sum(diagonal, axis=0, keepdims=True)
    diagonal_col = jnp.sum(diagonal, axis=1, keepdims=True)
    by_row, by_col = lax.rsqrt(diagonal_row), lax.rsqrt(diagonal_col)
    matrix = matrix * by_row * by_col
    shifted[...] = matrix
    low = 1.0 / jnp.max(diagonal_row, axis=1, keepdims=True)
    sums = jnp.sum(jnp.abs(matrix), axis=0, keepdims=True)
    high = jnp.maximum(jnp.max(sums, axis=1, keepdims=True), 1.0) * 1.01

    gap = 1.0 / (high - low)
    t_one = (high + low) * gap
    t_two = 2.0 * t_one * t_one - 1.0
    first = (t_one * identity) - (2.0 * gap) * matrix
    first_16 = first.astype(bf16)
    work[:width, :] = 2.0 * dot(first_16, first_16) - identity
    work[width:, :] = (4.0 * t_one / (t_two * (high + low))) * (t_one * identity + first)

    def more(carry):
        t, n = carry
        return jnp.logical_and(t[0, 0] < 8.0, n < 12)

    def double(carry):
        t, n = carry
        t_next = 2.0 * t * t - 1.0
        both = work[...]
        both_16 = both.astype(bf16)
        product = dot(both_16, both_16[:width])
        work[:width, :] = 2.0 * product[:width] - identity
        work[width:, :] = (2.0 * t / t_next) * (t * both[width:] + product[width:])
        return t_next, n + 1

    lax.while_loop(more, double, (t_two, 0))

    def unfinished(carry):
        size, n = carry
        return jnp.logical_and(size > GOOD * GOOD, n < 6)

    def refine(carry):
        _, n = carry
        inverse = work[width:, :]
        residual = identity - dot_three(shifted[...], inverse)
        work[width:, :] = inverse + dot(inverse.astype(bf16), residual.astype(bf16))
        return jnp.sum(residual * residual), n + 1

    size, _ = lax.while_loop(unfinished, refine, (jnp.float32(1e9), 0))

    @pl.when(jnp.logical_not(size <= GOOD * GOOD))
    def _():
        work[width:, :] = shifted[...]

        def eliminate(k, carry):
            value = work[width:, :]
            row = work[pl.ds(width + k, 1), :]
            at_col = col_ids == k
            col = jnp.sum(jnp.where(at_col, value, 0.0), axis=1, keepdims=True)
            pivot = 1.0 / jnp.sum(jnp.where(at_col[:1], row, 0.0), axis=1, keepdims=True)
            row = jnp.where(at_col[:1], pivot, row * pivot)
            value = jnp.where(at_col, 0.0, value) - col * row
            work[width:, :] = jnp.where(row_ids == k, row, value)
            return carry

        lax.fori_loop(0, width, eliminate, 0)

    inverse = work[width:, :]
    mixing[...] = (
        weight_beta / weight_gamma * identity
        + (weight_alpha - weight_beta / weight_gamma) * (inverse * by_row * by_col)
    )
    mixing_high, mixing_low = split(mixing[...])

    for i in range(rows // CHUNK):
        load(i).wait()
        part = pl.ds(i * CHUNK, CHUNK)
        high_part, low_part = split(held[part, :])
        ready[part, :] = dot(high_part, mixing_high) + (
            dot(high_part, mixing_low) + dot(low_part, mixing_high)
        )
        store(i).start()
    for i in range(rows // CHUNK):
        store(i).wait()


def applied(scale, gram, slab):
    rows, width = slab.shape
    dma = pltpu.SemaphoreType.DMA
    return pl.pallas_call(
        functools.partial(apply_kernel, scale),
        out_shape=jax.ShapeDtypeStruct((rows, width), f32),
        in_specs=[pl.BlockSpec(memory_space=pltpu.VMEM), pl.BlockSpec(memory_space=pl.ANY)],
        out_specs=pl.BlockSpec(memory_space=pl.ANY),
        scratch_shapes=[
            pltpu.VMEM((rows, width), f32),
            pltpu.VMEM((rows, width), f32),
            pltpu.VMEM((width, width), f32),
            pltpu.VMEM((2 * width, width), f32),
            pltpu.VMEM((width, width), f32),
            dma((rows // CHUNK,)),
            dma((rows // CHUNK,)),
        ],
        compiler_params=pltpu.CompilerParams(vmem_limit_bytes=VMEM_BYTES),
    )(gram, slab)


def local(slab):
    devices_all = lax.axis_size("rows") * lax.axis_size("group")
    scale = 0.5 * weight_gamma / (slab.shape[0] * devices_all)
    return applied(scale, reduced_gram(slab), slab)


def solution(mesh):
    placed = (P(("rows", "group"), None),)
    return jax.shard_map(
        local, mesh=mesh, in_specs=placed, out_specs=P(("rows", "group"), None), check_vma=False
    )
```

time: 388 us -> 57.2 us (0.15); the launches traced: 383 us -> 57 us
  waiting for transfers between devices: 154 us -> 0 us
  other arithmetic: 124 us -> 0 us
  matrix products: 61.4 us -> 0 us
  Pallas kernels: 0 us -> 56.9 us
  local copies, waits for them, and re-layouts: 27.5 us -> 0 us
  between operations: 16.4 us -> 0.17 us
    psum x2 -> x0, waiting for transfers between devices: 154 us -> none  [the longest x1 108 us: local(): within = lax.psum(partial_gram, 'rows')]
    another operation x17 -> x0, other arithmetic: 120 us -> none  [the longest x14 79.6 us: local(): lower = jnp.linalg.cholesky(scale * summed + identity)]
    pallas_call x0 -> x2, Pallas kernels: none -> 56.9 us  [the longest x1 34.2 us: reduced_gram(): pl.pallas_call(gram_kernel, out_shape=jax.ShapeDtypeStruct((2, HALF, TILE...]
    dot_general x3 -> x0, matrix products: 52.8 us -> none  [the longest x2 28.1 us: cross_product(): lax.dot_general(left, right, (((0,), (0,)), ((), ())), precision=lax.Prec...]
    another operation x34 -> x0, local copies, waits for them, and re-layouts: 14.5 us -> none
    dot_general x1 -> x0, local copies, waits for them, and re-layouts: 12.6 us -> none  [local(): jnp.dot(slab, mixing, precision=lax.Precision.HIGHEST, preferred_element_...]
    another operation x13 -> x0, matrix products: 8.59 us -> none  [the longest x7 5.43 us: local(): lax.linalg.triangular_solve(lower, identity, left_side=True, lower=True)]
  transfers between devices with their start and end apart: 2 -> 0, of which waited for: 2 -> 0; matrix products, arithmetic and copies ran while one was open for 0% -> 0% of each run, Pallas kernels for 0% -> 0%
where the time goes in v1:
time: 57.2 us; the launch traced here: 57 us
  Pallas kernels  56.9 us (99%)
    pallas_call x1, Pallas kernels, reduced_gram(): pl.pallas_call(gram_kernel, out_shape=jax.ShapeDtypeStruct((2, HALF, TILE...  34.2 us
    pallas_call x1, Pallas kernels, applied(): pl.pallas_call(functools.partial(apply_kernel, scale), out_shape=jax.Shap...  22.7 us

profile of v1, /device:TPU:1, one launch (start us, length us, event | category | flops | bytes accessed | tf_op | source)
XLA Modules:
  0.0 57.0 jit_solution(17029475208171924711)
XLA Ops:
  0.0 34.2 %shard_map.17.gram = f32[2,80,8,128]{3,2,1,0:T(8,128)} custom-call(f32[6144,512]{1,0:T(8,128)} %slab.3), custom_call_target="tpu_custom_call" | custom-call | tf_op jit(solution)/shard_map/pallas_call | solution.py:169
  34.2 22.7 %shard_map.18 = f32[6144,512]{1,0:T(8,128)} custom-call(f32[2,80,8,128]{3,2,1,0:T(8,128)} %shard_map.17.gram, f32[6144,512]{1,0:T(8,128)} %slab.3), custom_call_target="tpu_custom_call" | custom-call | tf_op jit(solution)/shard_map/pallas_call | solution.py:305

commit v2 on v1

--- a/solution.py
+++ b/solution.py
@@ -24,6 +24,7 @@
 BLOCK = 128
 TILE = 8
 CHUNK = 512
+PARTS = [1024, 1024, 1024, 1024, 1024, 512, 512]
 BLOCKS = [
     (0, 0), (0, 1), (0, 2), (0, 3), (1, 1),
     (1, 2), (1, 3), (2, 2), (2, 3), (3, 3),
@@ -31,8 +32,12 @@
 HALF = 5 * BLOCK // TILE
 STREAMS = [("xy", "z", 2, 0), ("yz", "x", 2, 32), ("zx", "y", 1, 64)]
 VMEM_BYTES = 56 * 2**20
-SHIFTS = [(i, j) for i in range(SIDE) for j in range(SIDE) if i or j]
+SHIFTS = sorted(
+    [(i, j) for i in range(SIDE) for j in range(SIDE) if i or j],
+    key=lambda shift: -sum(min(k, SIDE - k) for k in shift),
+)
 GOOD = 8e-3
+ROUNDS = 4
 
 f32, bf16 = jnp.float32, jnp.bfloat16
 
@@ -58,7 +63,7 @@
 
 def gram_kernel(
     slab, out, held, partial, packed, core_in, rs_a, rs_b, rs_c, ln_a, ln_b, ln_c, mine_a, mine_b,
-    mine_c, full, load_sem, core_sem, rs_send, rs_recv, ln_send, ln_recv, ag_send, ag_recv,
+    mine_c, full, load_sem, core_sem, back_sem, rs_send, rs_recv, ln_send, ln_recv, ag_send, ag_recv,
 ):
     rows = slab.shape[0]
     index = lax.axis_index("rows")
@@ -120,8 +125,8 @@
     rs, ln, mine = (rs_a, rs_b, rs_c), (ln_a, ln_b, ln_c), (mine_a, mine_b, mine_c)
     spots = [here[plane[0]] * SIDE + here[plane[1]] for plane, _, _, _ in STREAMS]
 
-    for s, (plane, _, units, first) in enumerate(STREAMS):
-        for k, (i, j) in enumerate(SHIFTS):
+    for k, (i, j) in enumerate(SHIFTS):
+        for s, (plane, _, units, first) in enumerate(STREAMS):
             spot = lax.rem(here[plane[0]] + i, SIDE) * SIDE + lax.rem(here[plane[1]] + j, SIDE)
             pltpu.make_async_remote_copy(
                 src_ref=packed.at[core, pl.ds(first + units * spot, units)], dst_ref=rs[s].at[k],
@@ -131,7 +136,7 @@
     for s, (plane, line, units, first) in enumerate(STREAMS):
         pltpu.make_async_copy(rs[s], rs[s], rs_recv.at[s]).wait()
         mine[s][...] = packed[core, pl.ds(first + units * spots[s], units)] + jnp.sum(rs[s][...], axis=0)
-        for k in range(SIDE - 1):
+        for k in (1, 0, 2):
             pltpu.make_async_remote_copy(
                 src_ref=mine[s], dst_ref=ln[s].at[k], send_sem=ln_send.at[s],
                 recv_sem=ln_recv.at[s], device_id=device({line: k + 1}), device_id_type=MESH,
@@ -145,20 +150,24 @@
                 src_ref=place, dst_ref=place, send_sem=ag_send.at[s], recv_sem=ag_recv.at[s],
                 device_id=device({plane[0]: i, plane[1]: j}), device_id_type=MESH,
             ).start()
+    backs = []
     for s, (plane, line, units, first) in enumerate(STREAMS):
         got = full.at[core, pl.ds(first, (PLANE - 1) * units)]
         pltpu.make_async_copy(got, got, ag_recv.at[s]).wait()
-    back = pltpu.make_async_remote_copy(
-        src_ref=full.at[core], dst_ref=full.at[core], send_sem=core_sem.at[2],
-        recv_sem=core_sem.at[3], device_id=sibling, device_id_type=MESH,
-    )
-    back.start()
+        stream = full.at[core, pl.ds(first, PLANE * units)]
+        back = pltpu.make_async_remote_copy(
+            src_ref=stream, dst_ref=stream, send_sem=back_sem.at[0, s], recv_sem=back_sem.at[1, s],
+            device_id=sibling, device_id_type=MESH,
+        )
+        back.start()
+        backs.append(back)
     for s, (plane, line, units, first) in enumerate(STREAMS):
         sent = full.at[core, pl.ds(first, (PLANE - 1) * units)]
         pltpu.make_async_copy(rs[s], rs[s], rs_send.at[s]).wait()
         pltpu.make_async_copy(ln[s], ln[s], ln_send.at[s]).wait()
         pltpu.make_async_copy(sent, sent, ag_send.at[s]).wait()
-    back.wait()
+    for back in backs:
+        back.wait()
     out[...] = full[...]
 
 
@@ -181,7 +190,8 @@
             *[unit(units) for _, _, units, _ in STREAMS],
             unit(2, HALF),
             dma((rows // CHUNK,)),
-            dma((4,)),
+            dma((2,)),
+            dma((2, 3)),
             *[dma((3,)) for _ in range(6)],
         ],
         compiler_params=pltpu.CompilerParams(
@@ -195,16 +205,8 @@
 ):
     rows, width = slab.shape
 
-    def load(i):
-        part = pl.ds(i * CHUNK, CHUNK)
-        return pltpu.make_async_copy(slab.at[part], held.at[part], load_sem.at[i])
-
-    def store(i):
-        part = pl.ds(i * CHUNK, CHUNK)
-        return pltpu.make_async_copy(ready.at[part], out.at[part], store_sem.at[i])
-
-    for i in range(rows // CHUNK):
-        load(i).start()
+    load = pltpu.make_async_copy(slab, held, load_sem)
+    load.start()
 
     row_ids = lax.broadcasted_iota(jnp.int32, (width, width), 0)
     col_ids = lax.broadcasted_iota(jnp.int32, (width, width), 1)
@@ -224,79 +226,82 @@
     shifted[...] = matrix
     low = 1.0 / jnp.max(diagonal_row, axis=1, keepdims=True)
     sums = jnp.sum(jnp.abs(matrix), axis=0, keepdims=True)
-    high = jnp.maximum(jnp.max(sums, axis=1, keepdims=True), 1.0) * 1.01
+    high = jnp.maximum(jnp.max(sums, axis=1, keepdims=True) * 1.01, 4.0 * low)
 
     gap = 1.0 / (high - low)
-    t_one = (high + low) * gap
-    t_two = 2.0 * t_one * t_one - 1.0
-    first = (t_one * identity) - (2.0 * gap) * matrix
-    first_16 = first.astype(bf16)
-    work[:width, :] = 2.0 * dot(first_16, first_16) - identity
-    work[width:, :] = (4.0 * t_one / (t_two * (high + low))) * (t_one * identity + first)
-
-    def more(carry):
-        t, n = carry
-        return jnp.logical_and(t[0, 0] < 8.0, n < 12)
-
-    def double(carry):
-        t, n = carry
+    t = (high + low) * gap
+    cheb = t * identity - (2.0 * gap) * matrix
+    cheb_16 = cheb.astype(bf16)
+    t_next = 2.0 * t * t - 1.0
+    inverse = (4.0 * t / (t_next * (high + low))) * (t * identity + cheb)
+    cheb = 2.0 * dot(cheb_16, cheb_16) - identity
+    t = t_next
+    for n in range(ROUNDS):
         t_next = 2.0 * t * t - 1.0
-        both = work[...]
-        both_16 = both.astype(bf16)
-        product = dot(both_16, both_16[:width])
-        work[:width, :] = 2.0 * product[:width] - identity
-        work[width:, :] = (2.0 * t / t_next) * (t * both[width:] + product[width:])
-        return t_next, n + 1
-
-    lax.while_loop(more, double, (t_two, 0))
+        cheb_16, inverse_16 = cheb.astype(bf16), inverse.astype(bf16)
+        if n < ROUNDS - 1:
+            product = dot(jnp.concatenate([inverse_16, cheb_16], 0), cheb_16)
+            cheb = 2.0 * product[width:] - identity
+            product = product[:width]
+        else:
+            product = dot(inverse_16, cheb_16)
+        inverse = (2.0 * t / t_next) * (t * inverse + product)
+        t = t_next
+
+    matrix_high, matrix_low = split(shifted[...])
+    inverse_16 = inverse.astype(bf16)
+    residual = identity - (dot(matrix_high, inverse_16) + dot(matrix_low, inverse_16))
+    inverse = inverse_16.astype(f32) + dot(inverse_16, residual.astype(bf16))
+
+    def refine(inverse):
+        residual = identity - dot_three(shifted[...], inverse)
+        work[...] = inverse + dot(inverse.astype(bf16), residual.astype(bf16))
+        return jnp.sum(residual * residual)
 
     def unfinished(carry):
         size, n = carry
-        return jnp.logical_and(size > GOOD * GOOD, n < 6)
-
-    def refine(carry):
-        _, n = carry
-        inverse = work[width:, :]
-        residual = identity - dot_three(shifted[...], inverse)
-        work[width:, :] = inverse + dot(inverse.astype(bf16), residual.astype(bf16))
-        return jnp.sum(residual * residual), n + 1
-
-    size, _ = lax.while_loop(unfinished, refine, (jnp.float32(1e9), 0))
+        return jnp.logical_and(size > GOOD * GOOD, n < 8)
+
+    size = refine(inverse)
+    size, _ = lax.while_loop(unfinished, lambda carry: (refine(work[...]), carry[1] + 1), (size, 0))
 
     @pl.when(jnp.logical_not(size <= GOOD * GOOD))
     def _():
-        work[width:, :] = shifted[...]
+        work[...] = shifted[...]
 
         def eliminate(k, carry):
-            value = work[width:, :]
-            row = work[pl.ds(width + k, 1), :]
+            value = work[...]
+            row = work[pl.ds(k, 1), :]
             at_col = col_ids == k
             col = jnp.sum(jnp.where(at_col, value, 0.0), axis=1, keepdims=True)
             pivot = 1.0 / jnp.sum(jnp.where(at_col[:1], row, 0.0), axis=1, keepdims=True)
             row = jnp.where(at_col[:1], pivot, row * pivot)
             value = jnp.where(at_col, 0.0, value) - col * row
-            work[width:, :] = jnp.where(row_ids == k, row, value)
+            work[...] = jnp.where(row_ids == k, row, value)
             return carry
 
         lax.fori_loop(0, width, eliminate, 0)
 
-    inverse = work[width:, :]
-    mixing[...] = (
-        weight_beta / weight_gamma * identity
-        + (weight_alpha - weight_beta / weight_gamma) * (inverse * by_row * by_col)
-    )
+    constant, factor = weight_beta / weight_gamma, weight_alpha - weight_beta / weight_gamma
+    inverse = work[...] * by_row * by_col
+    mixing[...] = constant * identity + factor * inverse
+
+    load.wait()
+
+    def store(n):
+        part = pl.ds(sum(PARTS[:n]), PARTS[n])
+        return pltpu.make_async_copy(ready.at[part], out.at[part], store_sem.at[n])
+
     mixing_high, mixing_low = split(mixing[...])
-
-    for i in range(rows // CHUNK):
-        load(i).wait()
-        part = pl.ds(i * CHUNK, CHUNK)
+    for n in range(len(PARTS)):
+        part = pl.ds(sum(PARTS[:n]), PARTS[n])
         high_part, low_part = split(held[part, :])
         ready[part, :] = dot(high_part, mixing_high) + (
             dot(high_part, mixing_low) + dot(low_part, mixing_high)
         )
-        store(i).start()
-    for i in range(rows // CHUNK):
-        store(i).wait()
+        store(n).start()
+    for n in range(len(PARTS)):
+        store(n).wait()
 
 
 def applied(scale, gram, slab):
@@ -311,10 +316,10 @@
             pltpu.VMEM((rows, width), f32),
             pltpu.VMEM((rows, width), f32),
             pltpu.VMEM((width, width), f32),
-            pltpu.VMEM((2 * width, width), f32),
             pltpu.VMEM((width, width), f32),
-            dma((rows // CHUNK,)),
-            dma((rows // CHUNK,)),
+            pltpu.VMEM((width, width), f32),
+            dma,
+            dma((len(PARTS),)),
         ],
         compiler_params=pltpu.CompilerParams(vmem_limit_bytes=VMEM_BYTES),
     )(gram, slab)

time: 57.2 us -> 51.2 us (0.90)
  Pallas kernels: 56.9 us -> 50.9 us
    pallas_call x1, Pallas kernels: 22.7 us -> 17.9 us  [applied(): pl.pallas_call(functools.partial(apply_kernel, scale), out_shape=jax.Shap...]
    pallas_call x1, Pallas kernels: 34.2 us -> 33.1 us  [reduced_gram(): pl.pallas_call(gram_kernel, out_shape=jax.ShapeDtypeStruct((2, HALF, TILE...]
where the time goes in v2:
time: 51.2 us; the launch traced here: 51.1 us
  Pallas kernels  50.9 us (99%)
    pallas_call x1, Pallas kernels, reduced_gram(): pl.pallas_call(gram_kernel, out_shape=jax.ShapeDtypeStruct((2, HALF, TILE...  33.1 us
    pallas_call x1, Pallas kernels, applied(): pl.pallas_call(functools.partial(apply_kernel, scale), out_shape=jax.Shap...  17.9 us

profile of v2, /device:TPU:1, one launch (start us, length us, event | category | flops | bytes accessed | tf_op | source)
XLA Modules:
  0.0 51.1 jit_solution(16412833070351052707)
XLA Ops:
  0.0 33.1 %shard_map.17.gram = f32[2,80,8,128]{3,2,1,0:T(8,128)} custom-call(f32[6144,512]{1,0:T(8,128)} %slab.3), custom_call_target="tpu_custom_call" | custom-call | tf_op jit(solution)/shard_map/pallas_call | solution.py:178
  33.1 17.9 %shard_map.18 = f32[6144,512]{1,0:T(8,128)} custom-call(f32[2,80,8,128]{3,2,1,0:T(8,128)} %shard_map.17.gram, f32[6144,512]{1,0:T(8,128)} %slab.3), custom_call_target="tpu_custom_call" | custom-call | tf_op jit(solution)/shard_map/pallas_call | solution.py:310

commit v3 on v2

--- a/solution.py
+++ b/solution.py
@@ -23,15 +23,15 @@
 PLANE = SIDE * SIDE
 BLOCK = 128
 TILE = 8
-CHUNK = 512
-PARTS = [1024, 1024, 1024, 1024, 1024, 512, 512]
+LOADS = [256, 512, 768, 1024, 1024, 1024, 1536]
+STORES = [1024, 1024, 1024, 1024, 1024, 512, 512]
 BLOCKS = [
     (0, 0), (0, 1), (0, 2), (0, 3), (1, 1),
     (1, 2), (1, 3), (2, 2), (2, 3), (3, 3),
 ]
 HALF = 5 * BLOCK // TILE
 STREAMS = [("xy", "z", 2, 0), ("yz", "x", 2, 32), ("zx", "y", 1, 64)]
-VMEM_BYTES = 56 * 2**20
+VMEM_BYTES = 50 * 2**20
 SHIFTS = sorted(
     [(i, j) for i in range(SIDE) for j in range(SIDE) if i or j],
     key=lambda shift: -sum(min(k, SIDE - k) for k in shift),
@@ -65,7 +65,6 @@
     slab, out, held, partial, packed, core_in, rs_a, rs_b, rs_c, ln_a, ln_b, ln_c, mine_a, mine_b,
     mine_c, full, load_sem, core_sem, back_sem, rs_send, rs_recv, ln_send, ln_recv, ag_send, ag_recv,
 ):
-    rows = slab.shape[0]
     index = lax.axis_index("rows")
     core = lax.rem(index, 2)
     here = {
@@ -81,10 +80,10 @@
     sibling = (index + 1 - 2 * core, here["x"])
 
     def load(i):
-        part = pl.ds(i * CHUNK, CHUNK)
+        part = pl.ds(sum(LOADS[:i]), LOADS[i])
         return pltpu.make_async_copy(slab.at[part], held.at[part], load_sem.at[i])
 
-    for i in range(rows // CHUNK):
+    for i in range(len(LOADS)):
         load(i).start()
 
     barrier = pltpu.get_barrier_semaphore()
@@ -99,9 +98,9 @@
         pl.semaphore_signal(barrier, inc=1, device_id=device(dict(shift)), device_id_type=MESH)
     pl.semaphore_signal(barrier, inc=1, device_id=sibling, device_id_type=MESH)
 
-    for i in range(rows // CHUNK):
+    for i in range(len(LOADS)):
         load(i).wait()
-        block = held[pl.ds(i * CHUNK, CHUNK), :]
+        block = held[pl.ds(sum(LOADS[:i]), LOADS[i]), :]
         high = block.astype(bf16)
         low = ((block - high.astype(f32)) * 2.0).astype(bf16)
         term = cross(jnp.concatenate([high, high], 0), jnp.concatenate([high, low], 0))
@@ -189,7 +188,7 @@
             *[unit(SIDE - 1, units) for _, _, units, _ in STREAMS],
             *[unit(units) for _, _, units, _ in STREAMS],
             unit(2, HALF),
-            dma((rows // CHUNK,)),
+            dma((len(LOADS),)),
             dma((2,)),
             dma((2, 3)),
             *[dma((3,)) for _ in range(6)],
@@ -251,6 +250,8 @@
     matrix_high, matrix_low = split(shifted[...])
     inverse_16 = inverse.astype(bf16)
     residual = identity - (dot(matrix_high, inverse_16) + dot(matrix_low, inverse_16))
+    residual_16 = residual.astype(bf16)
+    residual = residual + dot(residual_16, residual_16)
     inverse = inverse_16.astype(f32) + dot(inverse_16, residual.astype(bf16))
 
     def refine(inverse):
@@ -289,18 +290,18 @@
     load.wait()
 
     def store(n):
-        part = pl.ds(sum(PARTS[:n]), PARTS[n])
+        part = pl.ds(sum(STORES[:n]), STORES[n])
         return pltpu.make_async_copy(ready.at[part], out.at[part], store_sem.at[n])
 
     mixing_high, mixing_low = split(mixing[...])
-    for n in range(len(PARTS)):
-        part = pl.ds(sum(PARTS[:n]), PARTS[n])
+    for n in range(len(STORES)):
+        part = pl.ds(sum(STORES[:n]), STORES[n])
         high_part, low_part = split(held[part, :])
         ready[part, :] = dot(high_part, mixing_high) + (
             dot(high_part, mixing_low) + dot(low_part, mixing_high)
         )
         store(n).start()
-    for n in range(len(PARTS)):
+    for n in range(len(STORES)):
         store(n).wait()
 
 
@@ -319,7 +320,7 @@
             pltpu.VMEM((width, width), f32),
             pltpu.VMEM((width, width), f32),
             dma,
-            dma((len(PARTS),)),
+            dma((len(STORES),)),
         ],
         compiler_params=pltpu.CompilerParams(vmem_limit_bytes=VMEM_BYTES),
     )(gram, slab)

time: 51.2 us -> 49 us (0.957)
  Pallas kernels: 50.9 us -> 48.7 us
    pallas_call x1, Pallas kernels: 33.1 us -> 31.6 us  [reduced_gram(): pl.pallas_call(gram_kernel, out_shape=jax.ShapeDtypeStruct((2, HALF, TILE...]
    pallas_call x1, Pallas kernels: 17.9 us -> 17.1 us  [applied(): pl.pallas_call(functools.partial(apply_kernel, scale), out_shape=jax.Shap...]
where the time goes in v3:
time: 49 us; the launch traced here: 48.9 us
  Pallas kernels  48.7 us (99%)
    pallas_call x1, Pallas kernels, reduced_gram(): pl.pallas_call(gram_kernel, out_shape=jax.ShapeDtypeStruct((2, HALF, TILE...  31.6 us
    pallas_call x1, Pallas kernels, applied(): pl.pallas_call(functools.partial(apply_kernel, scale), out_shape=jax.Shap...  17.1 us

profile of v3, /device:TPU:1, one launch (start us, length us, event | category | flops | bytes accessed | tf_op | source)
XLA Modules:
  0.0 48.9 jit_solution(15763641263691899526)
XLA Ops:
  0.0 31.6 %shard_map.17.gram = f32[2,80,8,128]{3,2,1,0:T(8,128)S(1)} custom-call(f32[6144,512]{1,0:T(8,128)} %slab.3), custom_call_target="tpu_custom_call" | custom-call | tf_op jit(solution)/shard_map/pallas_call | solution.py:177
  31.6 17.1 %shard_map.18 = f32[6144,512]{1,0:T(8,128)} custom-call(f32[2,80,8,128]{3,2,1,0:T(8,128)S(1)} %shard_map.17.gram, f32[6144,512]{1,0:T(8,128)} %slab.3), custom_call_target="tpu_custom_call" | custom-call | tf_op jit(solution)/shard_map/pallas_call | solution.py:311

commit v4 on v3

--- a/solution.py
+++ b/solution.py
@@ -37,9 +37,12 @@
     key=lambda shift: -sum(min(k, SIDE - k) for k in shift),
 )
 GOOD = 8e-3
+LOW_SCALE = 512.0
+MOST_SPREAD = 1.5
+LEAST_COLUMN = 1 / 32
 ROUNDS = 4
 
-f32, bf16 = jnp.float32, jnp.bfloat16
+f32, bf16, f8 = jnp.float32, jnp.bfloat16, jnp.float8_e4m3fn
 
 
 def dot(left, right):
@@ -285,22 +288,51 @@
 
     constant, factor = weight_beta / weight_gamma, weight_alpha - weight_beta / weight_gamma
     inverse = work[...] * by_row * by_col
-    mixing[...] = constant * identity + factor * inverse
-
+    mixed = constant * identity + factor * inverse
+    inverse_diagonal = jnp.sum(inverse * identity, axis=0, keepdims=True)
+    mixing_diagonal = constant + factor * inverse_diagonal
+    off_diagonal = mixed * (1.0 - identity)
+    mixing[...] = mixed
+
+    spread = jnp.sum((diagonal_col - 1.0) * off_diagonal * off_diagonal)
+    trace, trace_inverse = jnp.sum(diagonal_row), jnp.sum(inverse_diagonal)
+    total = (
+        constant**2 * (trace - width)
+        + 2.0 * constant * factor * (width - trace_inverse)
+        + factor**2 * (trace_inverse - jnp.sum(inverse * inverse))
+    )
+    mild = jnp.logical_and(
+        spread <= MOST_SPREAD * total,
+        jnp.min(diagonal_row) >= 1.0 + weight_gamma * LEAST_COLUMN**2,
+    )
     load.wait()
 
     def store(n):
         part = pl.ds(sum(STORES[:n]), STORES[n])
         return pltpu.make_async_copy(ready.at[part], out.at[part], store_sem.at[n])
 
-    mixing_high, mixing_low = split(mixing[...])
-    for n in range(len(STORES)):
-        part = pl.ds(sum(STORES[:n]), STORES[n])
-        high_part, low_part = split(held[part, :])
-        ready[part, :] = dot(high_part, mixing_high) + (
-            dot(high_part, mixing_low) + dot(low_part, mixing_high)
-        )
-        store(n).start()
+    @pl.when(mild)
+    def _():
+        mixing_high, mixing_low = split(off_diagonal)
+        mixing_8 = (mixing_low.astype(f32) * LOW_SCALE).astype(f8)
+        for n in range(len(STORES)):
+            part = pl.ds(sum(STORES[:n]), STORES[n])
+            block = held[part, :]
+            high_part, low_part = split(block)
+            ready[part, :] = block * mixing_diagonal + (
+                dot(high_part, mixing_high)
+                + dot(low_part, mixing_high)
+                + dot(high_part.astype(f8), mixing_8) * (1.0 / LOW_SCALE)
+            )
+            store(n).start()
+
+    @pl.when(jnp.logical_not(mild))
+    def _():
+        for n in range(len(STORES)):
+            part = pl.ds(sum(STORES[:n]), STORES[n])
+            ready[part, :] = dot_three(held[part, :], mixing[...])
+            store(n).start()
+
     for n in range(len(STORES)):
         store(n).wait()
 

time: 49 us -> 49.6 us (1.012)
  Pallas kernels: 48.7 us -> 49.3 us
    pallas_call x1, Pallas kernels: 17.1 us -> 17.7 us  [applied(): pl.pallas_call(functools.partial(apply_kernel, scale), out_shape=jax.Shap...]
where the time goes in v4:
time: 49.6 us; the launch traced here: 49.5 us
  Pallas kernels  49.3 us (99%)
    pallas_call x1, Pallas kernels, reduced_gram(): pl.pallas_call(gram_kernel, out_shape=jax.ShapeDtypeStruct((2, HALF, TILE...  31.6 us
    pallas_call x1, Pallas kernels, applied(): pl.pallas_call(functools.partial(apply_kernel, scale), out_shape=jax.Shap...  17.7 us

profile of v4, /device:TPU:1, one launch (start us, length us, event | category | flops | bytes accessed | tf_op | source)
XLA Modules:
  0.0 49.5 jit_solution(9153054807239009007)
XLA Ops:
  0.0 31.6 %shard_map.17.gram = f32[2,80,8,128]{3,2,1,0:T(8,128)S(1)} custom-call(f32[6144,512]{1,0:T(8,128)} %slab.3), custom_call_target="tpu_custom_call" | custom-call | tf_op jit(solution)/shard_map/pallas_call | solution.py:180
  31.6 17.7 %shard_map.18 = f32[6144,512]{1,0:T(8,128)} custom-call(f32[2,80,8,128]{3,2,1,0:T(8,128)S(1)} %shard_map.17.gram, f32[6144,512]{1,0:T(8,128)} %slab.3), custom_call_target="tpu_custom_call" | custom-call | tf_op jit(solution)/shard_map/pallas_call | solution.py:343
